TPU v7x, 32 devices: a whole 2x2x4 slice. The times are simulated.
32 devices in a mesh: section: 2 (over core), dp: 16 (over z, y, x).
Axes of the slice: x: 2, y: 2, z: 4, core: 2. Of those that a mesh axis runs over, the one named last changes fastest.
Arguments:
- embeddings: bfloat16 [2, 16384, 512], P('section', 'dp'), may hold values from -6 to 6
- cotangent: bfloat16 [16384, 512], P('dp'), may hold values from -6 to 6
- source_lengths: int32 [32, 8], P('dp'), may hold values from 1 to 256, 512 in all within a row
- target_lengths: int32 [32, 8], P('dp'), may hold values from 1 to 256, 512 in all within a row
- self_routes: int32 [2, 16384, 2], P('section', 'dp'), may hold values from 0 to 7, all different within a row
- cross_routes: int32 [16384, 2], P('dp'), may hold values from 0 to 7, all different within a row
- attend_gain: float32 [2, 512], P('section'), may hold values from 0.5 to 1.5
- attend_bias: float32 [2, 512], P('section'), may hold values from -1.25 to 1.25
- self_router: bfloat16 [2, 512, 8], P('section'), may hold values from -0.1875 to 0.1875
- query_weight: bfloat16 [2, 512, 512], P('section'), may hold values from -0.25 to 0.25
- key_weight: bfloat16 [2, 512, 64], P('section'), may hold values from -0.25 to 0.25
- value_weight: bfloat16 [2, 512, 64], P('section'), may hold values from -0.25 to 0.25
- output_weight: bfloat16 [2, 512, 512], P('section'), may hold values from -4 to 4
- feed_gain: float32 [2, 512], P('section'), may hold values from 0.5 to 1.5
- feed_bias: float32 [2, 512], P('section'), may hold values from -1.25 to 1.25
- expand_weight: bfloat16 [2, 512, 2048], P('section'), may hold values from -0.25 to 0.25
- expand_bias: float32 [2, 2048], P('section'), may hold values from -1.75 to 1.75
- reduce_weight: bfloat16 [2, 2048, 512], P('section'), may hold values from -0.125 to 0.125
- reduce_bias: float32 [2, 512], P('section'), may hold values from -1.75 to 1.75
- cross_gain: float32 [512], replicated, may hold values from 0.5 to 1.5
- cross_bias: float32 [512], replicated, may hold values from -1.25 to 1.25
- cross_router: bfloat16 [512, 8], replicated, may hold values from -0.1875 to 0.1875
- cross_query: bfloat16 [512, 512], replicated, may hold values from -0.25 to 0.25
- cross_key: bfloat16 [512, 64], replicated, may hold values from -0.25 to 0.25
- cross_value: bfloat16 [512, 64], replicated, may hold values from -0.25 to 0.25
- cross_output: bfloat16 [512, 512], replicated, may hold values from -4 to 4
Outputs:
- activations: bfloat16 [2, 16384, 512], P('section', 'dp')
- input_grads: float32 [2, 16384, 512], P('section', 'dp')
- grad_attend_gain: float32 [2, 512], P('section')
- grad_attend_bias: float32 [2, 512], P('section')
- grad_self_router: float32 [2, 512, 8], P('section')
- grad_query_weight: float32 [2, 512, 512], P('section')
- grad_key_weight: float32 [2, 512, 64], P('section')
- grad_value_weight: float32 [2, 512, 64], P('section')
- grad_output_weight: float32 [2, 512, 512], P('section')
- grad_feed_gain: float32 [2, 512], P('section')
- grad_feed_bias: float32 [2, 512], P('section')
- grad_expand_weight: float32 [2, 512, 2048], P('section')
- grad_expand_bias: float32 [2, 2048], P('section')
- grad_reduce_weight: float32 [2, 2048, 512], P('section')
- grad_reduce_bias: float32 [2, 512], P('section')
- grad_cross_gain: float32 [512], replicated
- grad_cross_bias: float32 [512], replicated
- grad_cross_router: float32 [512, 8], replicated
- grad_cross_query: float32 [512, 512], replicated
- grad_cross_key: float32 [512, 64], replicated
- grad_cross_value: float32 [512, 64], replicated
- grad_cross_output: float32 [512, 512], replicated
Inputs may be any that keep to these rules, and one draw needn't show every extreme that they name: `source_lengths`: each row of 8 sentence lengths sums to 512, and its longest sentence has exactly 256 tokens. `target_lengths`: each row of 8 sentence lengths sums to 512, and its longest sentence has exactly 256 tokens. `self_routes`: each token names 2 different experts. `cross_routes`: each token names 2 different experts.
All inputs are finite; a program needn't handle non-finite values.
Results may differ from a plain program's by a relative error of at most 0.022.
The roundings to bfloat16 on the way count: a program that leaves them out, or rounds other values in their place, can miss the bound.
Values may be sent and summed in bfloat16 or wider, within the bound.
A program may use at most 192 MiB of HBM per device.

v0:
```python
import functools
import math

import jax
import jax.numpy as jnp
from jax import lax
from jax.experimental import pallas as pl
from jax.experimental.pallas import tpu as pltpu
from jax.sharding import PartitionSpec as P

EPSILON = 1e-05
SCORE_SCALE = 0.125
MASKED_SCORE = -1000000000.0
F32 = jnp.float32
BF16 = jnp.bfloat16
T = 512
D = 512
FF = 2048
PAIR = 128
CH = 512
PARTS = 2
PART = FF // PARTS
NARROW = 160
MESH = pl.DeviceIdType.MESH


def dot(a, b):
    return lax.dot_general(a, b, (((1,), (0,)), ((), ())), preferred_element_type=F32)


def dot_nt(a, b):
    return lax.dot_general(a, b, (((1,), (1,)), ((), ())), preferred_element_type=F32)


def dot_tn(a, b):
    return lax.dot_general(a, b, (((0,), (0,)), ((), ())), preferred_element_type=F32)


def iota(shape, axis):
    return lax.broadcasted_iota(jnp.int32, shape, axis)


def norm_parts(v):
    centred = v - jnp.mean(v, axis=-1, keepdims=True)
    spread = jnp.mean(centred * centred, axis=-1, keepdims=True)
    return centred, lax.rsqrt(spread + EPSILON)


def norm(v, gain, bias):
    centred, scale = norm_parts(v)
    return centred * scale * gain + bias


def norm_back(dn, v, gain):
    centred, scale = norm_parts(v)
    unit = centred * scale
    dgain = jnp.sum(dn * unit, axis=0, keepdims=True)
    dbias = jnp.sum(dn, axis=0, keepdims=True)
    dunit = dn * gain
    first = jnp.mean(dunit, axis=-1, keepdims=True)
    second = jnp.mean(dunit * unit, axis=-1, keepdims=True)
    return scale * (dunit - first - unit * second), dgain, dbias


def ids_of(ends, shape, axis):
    places = iota(shape, axis)
    total = jnp.zeros(shape, jnp.int32)
    for end in ends:
        total = total + (places >= end).astype(jnp.int32)
    return total


def ends_of(lengths):
    ends, total = [], jnp.int32(0)
    for length in lengths:
        total = total + length
        ends.append(total)
    return ends


def same_of(key_ends, query_ends):
    return ids_of(key_ends, (T, 1), 0) == ids_of(query_ends, (1, T), 1)


def earlier():
    return iota((T, T), 0) <= iota((T, T), 1)


def chosen(expert, block):
    return expert == (iota((T, PAIR), 1) // 64 + 2 * block).astype(F32)


def laid_out(row):
    return jnp.broadcast_to(row, (PAIR, T)).T


def mixture_fwd(a, s, experts, w, allowed, kept, with_out=True):
    wq, wk2, wv2, wkv, wr2, wo = w
    q = dot(a, wq[...])
    logits = dot_nt(a, wr2[...])
    kk = dot_nt(s, wk2[...]).astype(BF16)
    vv = dot_nt(s, wv2[...]).astype(BF16)
    kept["kk"][...] = kk
    kept["vv"][...] = vv
    lanes = iota((T, PAIR), 1).astype(F32)
    raised = [
        jnp.exp(jnp.sum(jnp.where(lanes == e, logits, 0.0), axis=-1, keepdims=True))
        for e in experts
    ]
    total = raised[0] + raised[1]
    gated = [jnp.zeros((T, PAIR), F32) for _ in range(4)]
    for r in range(2):
        gate = raised[r] / total
        kept["gate"][r] = jnp.broadcast_to(gate, (T, PAIR))
        qs = jnp.zeros((T, PAIR), F32)
        for b in range(4):
            qs = jnp.where(chosen(experts[r], b), q[:, b * PAIR : (b + 1) * PAIR], qs)
        qs = qs.astype(BF16)
        kept["qs"][r] = qs
        scores = jnp.where(allowed, dot_nt(kk, qs) * SCORE_SCALE, MASKED_SCORE)
        top = jnp.max(scores, axis=0, keepdims=True)
        p = jnp.exp(scores - top)
        inverse = 1.0 / jnp.sum(p, axis=0, keepdims=True)
        kept["top"][r : r + 1] = top
        kept["inv"][r : r + 1] = inverse
        chance = (p * inverse).astype(BF16)
        mixed = dot_tn(vv, chance).T
        kept["mixed"][r] = mixed
        weighted = gate * mixed
        for b in range(4):
            gated[b] = jnp.where(chosen(experts[r], b), weighted, gated[b])
    for b in range(4):
        kept["gated"][:, b * PAIR : (b + 1) * PAIR] = gated[b].astype(BF16)
    if with_out:
        return dot(kept["gated"][...], wo[...])


def mixture_bwd(dy, a, s, experts, w, allowed, kept, wide, base, narrow, nbase, mark):
    wq, wk2, wv2, wkv, wr2, wo = w
    wide[base + D : base + 2 * D, :] = dot_tn(kept["gated"][...], dy).astype(BF16)
    dgated = dot_nt(dy, wo[...]).astype(BF16).astype(F32)
    kk, vv = kept["kk"][...], kept["vv"][...]
    lanes = iota((T, PAIR), 1)
    dkk = jnp.zeros((T, PAIR), F32)
    dvv = jnp.zeros((T, PAIR), F32)
    dgates, gates, dqs = [], [], []
    for r in range(2):
        own = jnp.zeros((T, PAIR), F32)
        for b in range(4):
            own = jnp.where(chosen(experts[r], b), dgated[:, b * PAIR : (b + 1) * PAIR], own)
        gate = kept["gate"][r]
        gates.append(gate)
        dgates.append(jnp.sum(own * kept["mixed"][r], axis=-1, keepdims=True))
        dmixed = (gate * own).astype(BF16)
        qs = kept["qs"][r]
        scores = jnp.where(allowed, dot_nt(kk, qs) * SCORE_SCALE, MASKED_SCORE)
        p = jnp.exp(scores - kept["top"][r : r + 1]) * kept["inv"][r : r + 1]
        dp = dot_nt(vv, dmixed)
        both = jnp.sum(p * dp, axis=0, keepdims=True)
        ds = (p * (dp - both)).astype(BF16)
        dkk = dkk + dot(ds, qs)
        dvv = dvv + dot(p.astype(BF16), dmixed)
        dqs.append((dot_tn(kk, ds) * SCORE_SCALE).T)
        mark()
    dq = []
    for b in range(4):
        part = jnp.zeros((T, PAIR), F32)
        for r in range(2):
            part = jnp.where(chosen(experts[r], b), dqs[r], part)
        dq.append(part.astype(BF16))
    dq = jnp.concatenate(dq, axis=1)
    dk = (dkk + pltpu.roll(dkk, 64, 1)) * SCORE_SCALE
    dv = dvv + pltpu.roll(dvv, 64, 1)
    dkv = jnp.where(lanes < 64, dk, dv).astype(BF16)
    mean = gates[0] * dgates[0] + gates[1] * dgates[1]
    dl = jnp.zeros((T, PAIR), F32)
    for r in range(2):
        dl = jnp.where(((lanes % 8).astype(F32) == experts[r]) & (lanes < 16), gates[r] * (dgates[r] - mean), dl)
    high = dl.astype(BF16).astype(F32)
    dl = jnp.where(lanes < 8, high, dl - high).astype(BF16)
    wide[base : base + D, :] = dot_tn(a, dq).astype(BF16)
    narrow[nbase : nbase + PAIR, :] = dot_tn(dkv, s).astype(BF16)
    dwr = dot_tn(dl, a)
    dwr = dwr[0:8] + dwr[8:16]
    narrow[nbase + PAIR : nbase + PAIR + 16, :] = jnp.concatenate([dwr, jnp.zeros((8, D), F32)], axis=0).astype(BF16)
    da = dot_nt(dq, wq[...]) + dot(dl, wr2[...])
    ds = dot(dkv, wkv[...])
    return da, ds


C0, C1 = 0.7978845608028654, 0.044715


def gelu(pre):
    half = 0.5 * jnp.tanh(C0 * (pre + C1 * pre * pre * pre)) + 0.5
    return pre * half


def gelu_both(pre):
    square = pre * pre
    t = jnp.tanh(C0 * pre * (1.0 + C1 * square))
    half = 0.5 * t + 0.5
    slope = half + 0.5 * pre * (1.0 - t * t) * (C0 * (1.0 + 3.0 * C1 * square))
    return pre * half, slope


def expand_step(j, f, we, p):
    at = pl.multiple_of(j * CH, CH)
    return dot(f[...], we[:, pl.ds(at, CH)]) + p[pl.ds(5 + j, 1), :]


def feed_fwd(pairs, we, p, wr):
    def step(j, carry):
        at = pl.multiple_of(j * CH, CH)
        for f, acc in pairs:
            hidden = gelu(expand_step(j, f, we, p)).astype(BF16)
            acc[...] += dot(hidden, wr[pl.ds(at, CH), :])
        return carry

    lax.fori_loop(0, FF // CH, step, 0)


def small_rows(rows, count=16):
    places = iota((count, D), 0)
    out = jnp.zeros((count, D), F32)
    for i, row in enumerate(rows):
        out = jnp.where(places == i, row, out)
    return out


KEPT = (
    ("kk", (T, PAIR), BF16),
    ("vv", (T, PAIR), BF16),
    ("gate", (2, T, PAIR), F32),
    ("qs", (2, T, PAIR), BF16),
    ("top", (8, T), F32),
    ("inv", (8, T), F32),
    ("mixed", (2, T, PAIR), F32),
    ("gated", (T, D), BF16),
)


class Here:
    def __init__(self, n):
        self.bits = n.bit_length() - 1
        self.sec = lax.axis_index("section")
        self.rank = lax.axis_index("dp")

    def side(self, b):
        return lax.rem(self.rank // (1 << b), 2)

    def partner(self, b):
        return (self.sec, self.rank + (1 - 2 * self.side(b)) * (1 << b))

    def twin(self):
        return (1 - self.sec, self.rank)


def scattered(n):
    return min(4, n.bit_length() - 1)


def up(rows, n):
    unit = 16 << scattered(n)
    return -(-rows // unit) * unit


PLAN = (
    ((1, (1, 0, 2, 3)), (2, (2, 0, 1, 3)), (1, (0, 3, 1, 2))),
    ((1, (0, 1, 2, 3)), (2, (0, 1, 2, 3)), (1, (1, 3, 2, 0))),
    ((1, (1, 0, 2, 3)), (1, (3, 0, 1, 2))),
    ((2, (0, 1, 2, 3)), (1, (1, 3, 0, 2)), (1, (0, 1, 2, 3))),
    ((1, (1, 0, 2, 3)), (2, (2, 0, 1, 3)), (1, (0, 1, 2, 3))),
    ((1, (1, 0, 2, 3)), (1, (2, 1, 0, 3))),
    ((1, (1, 0, 3, 2)), (1, (0, 1, 2, 3)), (1, (0, 1, 2, 3))),
)
MARKS = (
    (),
    (),
    (),
    (0,),
    (2,),
    (1, 3, 5, 2, 4, 0, 6),
    (7, 11, 12, 13),
    (9,),
    (3, 0, 2, 8, 5),
    (4, 10),
    (14, 15, 11, 1),
    (12, 6, 3),
    (7, 8, 2, 9, 10, 0, 5, 13, 4, 11, 14),
    (
        15, 1, 6, 16, 12, 17, 3, 18, 7, 9, 8, 5, 2, 10, 13, 0, 14, 11, 15, 4, 7, 1, 9, 6,
        17, 16, 3, 13, 12, 8, 2, 0, 10, 18, 14, 5, 17, 7, 11, 15, 9, 4, 16, 3, 18, 1, 0, 7,
        5, 6, 9, 13, 17, 3, 12, 1, 8, 7, 4, 18, 0, 2, 6, 10, 3, 14, 11, 0, 4, 15, 8, 1,
        3, 16, 10, 11, 2, 5, 6, 8, 2, 9, 10, 13, 17, 12, 5, 4, 11, 5, 6, 4, 1, 6, 7, 16,
        9, 18, 13, 14, 12, 1, 15, 8, 7, 17, 9, 16, 18, 11, 14, 10, 8, 13, 17, 11, 16, 18, 10, 12,
        15, 17, 14, 18, 15, 13, 16, 13, 14, 12, 17, 14, 12, 15, 16, 17, 18, 15, 16, 18,
    ),
)


def streams_of(group, half, n):
    bits = n.bit_length() - 1
    shares = sum(share for share, _ in PLAN[group])
    out, at = [], 0
    for share, order in PLAN[group]:
        rows = half * share // shares
        piece = rows >> scattered(n)
        lands = rows - piece + (bits - scattered(n)) * piece
        out.append((at, rows, lands, [b for b in order if b < bits] + list(range(4, bits))))
        at += rows
    return out


def add_rows(dst, at, src, start, rows):
    block = math.gcd(rows, 128)

    def step(i, carry):
        to = pl.ds(pl.multiple_of(at + i * block, 16), block)
        dst[to, :] = dst[to, :] + src[pl.ds(pl.multiple_of(start + i * block, 16), block), :]
        return carry

    lax.fori_loop(0, rows // block, step, 0)


def sum_steps(here, g, twin_in, ring_in, send, recv, free, half, first, rows, order, owner):
    def remote(i, src, dst, device):
        return pltpu.make_async_remote_copy(
            src_ref=src, dst_ref=dst, send_sem=send, recv_sem=recv.at[i],
            device_id=device, device_id_type=MESH,
        )

    def rows_at(at, count):
        return g.at[pl.ds(pl.multiple_of(at, 16), count)]

    def signal(i, device):
        pl.semaphore_signal(free.at[i], inc=1, device_id=device, device_id_type=MESH)

    def summed(copy, credit, device, at, source, start, length):
        def end():
            copy.wait()
            if credit is not None:
                signal(credit, device)
            add_rows(g, at, source, start, length)

        return end

    def after(credit, copy):
        def start():
            pl.semaphore_wait(free.at[credit], 1)
            copy.start()

        return start

    mine = here.sec * half + first
    other = (1 - here.sec) * half + first
    copies = 0
    copy = remote(copies, rows_at(other, rows), twin_in.at[pl.ds(first, rows)], here.twin())
    moves = [(copy.start, summed(copy, 0, here.twin(), mine, twin_in, first, rows))]
    at, length, landing, trail = mine, rows, 0, []
    for step, b in enumerate(order):
        copies += 1
        partner = here.partner(b)
        if step >= 4:
            copy = remote(copies, rows_at(at, length), ring_in.at[pl.ds(landing, length)], partner)
            moves.append((copy.start, summed(copy, None, partner, at, ring_in, landing, length)))
            landing += length
            continue
        length //= 2
        side = here.side(b)
        keep, give = at + side * length, at + (1 - side) * length
        copy = remote(copies, rows_at(give, length), ring_in.at[pl.ds(landing, length)], partner)
        moves.append((copy.start, summed(copy, 1 + step, partner, keep, ring_in, landing, length)))
        trail.append((b, at, length))
        at, landing = keep, landing + length
    for step, (b, before, length) in reversed(list(enumerate(trail))):
        copies += 1
        copy = remote(copies, rows_at(at, length), rows_at(at, length), here.partner(b))
        moves.append((after(1 + step, copy), copy.wait))
        at = before
    copies += 1
    copy = remote(copies, rows_at(mine, rows), rows_at(mine, rows), here.twin())
    if owner is None:
        moves.append((after(0, copy), copy.wait))
    else:
        gives = here.sec != owner

        def start():
            pl.semaphore_wait(free.at[0], 1)
            pl.when(gives)(copy.start)

        def end():
            pl.when(gives)(copy.wait_send)
            pl.when(jnp.logical_not(gives))(copy.wait_recv)

        moves.append((start, end))
    ends = [end for _, end in moves]
    starts = [start for start, _ in moves[1:]]

    def both(end, start):
        def step():
            end()
            start()

        return step

    return [moves[0][0]] + [both(end, start) for end, start in zip(ends, starts)] + [ends[-1]]


def fused(n, halves, sents, *refs):
    (
        sl, tl, routes, xroutes, ag, ab, fg, fb, rb, eb, wk, wv, wrt, cg, cb, xwk, xwv, xwrt,
        emb, cot, wq, wo, we, wr, xwq, xwo,
        act_out, gin_out, gff_out, gat_out, gx_out,
        x_v, p_v, xp_v, sm_v, xsm_v, wq_v, wo_v, we_v, wr_v, cot_v, xwq_v, xwo_v,
        wsm, kept_refs, low_v, mid_v, mem_v, stage_v, f_v, ft_v, totals, deb, out_v,
        gff, gx_v, ge_v, gd_v, twin_in, ring_in, sum_send, sum_recv, sum_free,
        own_sem, in_send, in_recv, out_sem, out_send, out_recv,
    ) = refs
    here = Here(n)
    sec = here.sec
    acc, dacc = totals.at[0], totals.at[1]
    barrier = pltpu.get_barrier_semaphore()
    pl.semaphore_signal(barrier, inc=1, device_id=here.twin(), device_id_type=MESH)
    for b in range(here.bits):
        pl.semaphore_signal(barrier, inc=1, device_id=here.partner(b), device_id_type=MESH)

    def slot(ref, which):
        return ref.at[pl.ds(pl.multiple_of(which * T, T), T)]

    def remote(src, dst, send, recv):
        return pltpu.make_async_remote_copy(
            src_ref=src, dst_ref=dst, send_sem=send, recv_sem=recv, device_id=here.twin(), device_id_type=MESH
        )

    local = {}
    for i, (name, src, dst) in enumerate((
        ("x_oth", slot(emb, 1 - sec), x_v.at[2]), ("x", slot(emb, sec), x_v.at[sec]), ("wq", wq, wq_v.at[sec]),
        ("wo", wo, wo_v.at[sec]), ("we", we, we_v.at[sec]), ("wr", wr, wr_v.at[sec]),
        ("xwq", xwq, xwq_v), ("xwo", xwo, xwo_v), ("cot", slot(cot, sec), cot_v),
    )):
        local[name] = pltpu.make_async_copy(src, dst, own_sem.at[i])
        local[name].start()

    def need(*names):
        for name in names:
            local[name].wait()

    own_at = pl.multiple_of(sec * T, T)
    p_v[sec] = small_rows(
        [ref[...] for ref in (ag, ab, fg, fb, rb)]
        + [eb[:, i * D : (i + 1) * D] for i in range(FF // D)]
        + [routes[r : r + 1, m * T : (m + 1) * T].astype(F32) for m in range(2) for r in range(2)]
    )
    xp_v[...] = small_rows(
        [cg[...], cb[...]] + [xroutes[r : r + 1, pl.ds(own_at, T)].astype(F32) for r in range(2)]
    )

    def pack(wk, wv, wrt):
        router = wrt[...].astype(F32)
        tail = jnp.concatenate([router, router, jnp.zeros((16, D), F32)], axis=0).astype(BF16)
        return jnp.concatenate([wk[...], wv[...], tail], axis=0)

    sm_v[sec] = pack(wk, wv, wrt)
    xsm_v[...] = pack(xwk, xwv, xwrt)

    def lay_small(l, ref):
        for i in range(2):
            half = ref[64 * i : 64 * i + 64]
            wsm[l, i] = jnp.concatenate([half, half], axis=0)
        wsm[l, 2] = jnp.concatenate([ref[128:144], jnp.zeros((112, D), BF16)], axis=0)

    def weights(l, small):
        return (
            wq_v.at[l], wsm.at[l, 0], wsm.at[l, 1], small.at[pl.ds(0, PAIR)], wsm.at[l, 2], wo_v.at[l],
        )

    def p(l, i):
        return p_v[l, i : i + 1, :]

    def experts_of(ref, first):
        return [laid_out(ref[first + r : first + r + 1, :]) for r in range(2)]

    kept = [dict(zip([k[0] for k in KEPT], k)) for k in kept_refs]

    lay_small(sec, sm_v.at[sec])

    def own_middle(i, carry):
        row = jnp.where(i == 0, 1 - sec, sec)
        ends = ends_of([jnp.where(sec == 0, sl[row, i], tl[row, i]) for i in range(sents)])
        allowed = same_of(ends, ends) & (earlier() | (sec == 0))
        x = x_v[jnp.where(i == 0, 2, sec)].astype(F32)
        a = norm(x, p(sec, 0), p(sec, 1)).astype(BF16)
        at = 9 + 2 * row
        experts = [laid_out(p_v[sec, pl.ds(at + r, 1), :]) for r in range(2)]
        totals[1 - i] = x + mixture_fwd(a, a, experts, weights(sec, sm_v.at[sec]), allowed, kept[0])

        @pl.when(i == 0)
        def _():
            pl.semaphore_wait(barrier, here.bits + 1)
            for name in ("p", "sm", "we", "wr", "wq", "wo", "x"):
                swaps[name].start()

        return carry

    swaps = {}
    for i, (name, src, dst) in enumerate((
        ("p", p_v.at[sec], p_v), ("sm", sm_v.at[sec], sm_v), ("we", we, we_v), ("wr", wr, wr_v), ("wq", wq, wq_v),
        ("wo", wo, wo_v), ("x", slot(emb, 1 - sec), x_v),
    )):
        swaps[name] = remote(src, dst.at[sec], in_send.at[i], in_recv.at[i])

    def swapped(*names):
        for name in names:
            swaps[name].wait()

    need("x_oth", "x", "wq", "wo")
    lax.fori_loop(0, 2, own_middle, 0)
    need("we", "wr")
    middle_away = remote(dacc, mid_v.at[1], in_send.at[7], in_recv.at[7])
    memory_away = remote(stage_v, mem_v, in_send.at[8], in_recv.at[8])

    @pl.when(sec == 0)
    def _():
        for f, total in ((f_v, acc), (stage_v, dacc)):
            middle = total[...]
            f[...] = norm(middle, p(0, 2), p(0, 3)).astype(BF16)
            total[...] = middle + p(0, 4)
        feed_fwd(((f_v, acc), (stage_v, dacc)), we_v.at[0], p_v.at[0], wr_v.at[0])
        stage_v[...] = dacc[...].astype(BF16)
        memory_away.start()
        mem_v[...] = acc[...].astype(BF16)

    @pl.when(sec == 1)
    def _():
        middle_away.start()
        mid_v[1] = acc[...]

    need("xwq", "xwo", "cot")
    lay_small(2, xsm_v)

    @pl.when(sec == 0)
    def _():
        middle_away.wait_recv()
        memory_away.wait_send()

    @pl.when(sec == 1)
    def _():
        memory_away.wait_recv()
        middle_away.wait_send()

    finals = []

    def hand_out(start, end):
        start()
        finals.append(end)

    memory_out = [
        pltpu.make_async_copy(ref, act_out.at[pl.ds(m * T, T)], out_sem.at[m]) for m, ref in enumerate((mem_v, stage_v))
    ]

    @pl.when(sec == 0)
    def _():
        for copy in memory_out:
            copy.start()

    s_ends, t_ends = (ends_of([ref[sec, i] for i in range(sents)]) for ref in (sl, tl))
    xw = (xwq_v, wsm.at[2, 0], wsm.at[2, 1], xsm_v.at[pl.ds(0, PAIR)], wsm.at[2, 2], xwo_v)
    c = norm(mid_v[1], xp_v[0:1, :], xp_v[1:2, :]).astype(BF16)
    low_v[1] = c
    mid_v[2] = mid_v[1] + mixture_fwd(c, mem_v[...], experts_of(xp_v, 2), xw, same_of(s_ends, t_ends), kept[1])

    groups = (
        (gff.at[1, 0], 1), (gff.at[1, 1], 1), (gx_v, None), (gff.at[0, 0], 0), (gff.at[0, 1], 0), (ge_v, 0), (gd_v, None),
    )
    live, waiting, state = {}, {}, {"stream": 0, "landed": 0, "mark": 0}
    steps_in_all = here.bits + scattered(n) + 3

    def done(i):
        pairs = {
            0: [(1, gff.at[1, 0], gff_out.at[pl.ds(0, FF)], 3)],
            1: [(1, gff.at[1, 1], gff_out.at[pl.ds(FF, FF)], 4)],
            2: [(None, gx_v, gx_out.at[pl.ds(0, 2 * D)], 5)],
            3: [(0, gff.at[0, 0], gff_out.at[pl.ds(0, FF)], 6)],
            4: [(0, gff.at[0, 1], gff_out.at[pl.ds(FF, FF)], 7)],
            5: [(0, ge_v, gat_out.at[pl.ds(0, 2 * D)], 8)],
            6: [(1, gd_v.at[pl.ds(0, 2 * D)], gat_out.at[pl.ds(0, 2 * D)], 9)]
            + [(l, gd_v.at[pl.ds(2 * D + l * NARROW, NARROW)], gat_out.at[pl.ds(2 * D, NARROW)], 10 + l) for l in range(2)]
            + [(None, gd_v.at[pl.ds(2 * D + 2 * NARROW, NARROW)], gx_out.at[pl.ds(2 * D, NARROW)], 12)],
        }
        for owner, src, dst, sem in pairs[i]:
            copy = pltpu.make_async_copy(src, dst, out_sem.at[sem])
            if owner is None:
                copy.start()
                finals.append(copy.wait)
            else:
                pl.when(sec == owner)(copy.start)
                finals.append(functools.partial(pl.when(sec == owner), copy.wait))

    def advance(k):
        i, steps = live[k]
        steps.pop(0)()
        if not steps:
            del live[k]
            if all(entry[0] != i for entry in live.values()):
                done(i)

    for i, (g, owner) in enumerate(groups):
        for first, rows, lands, order in streams_of(i, halves[i], n):
            k = state["stream"]
            steps = sum_steps(
                here, g, twin_in.at[i % 2], ring_in.at[pl.ds(state["landed"], lands)],
                sum_send.at[k], sum_recv.at[k], sum_free.at[k], halves[i], first, rows, order, owner,
            )
            waiting[k] = [i, steps]
            state["stream"] += 1
            state["landed"] += lands

    def begin(i):
        for k in [k for k in live if live[k][0] == i - 1 and len(live[k][1]) == steps_in_all - 1]:
            advance(k)
        for k in [k for k in waiting if waiting[k][0] == i]:
            live[k] = waiting.pop(k)
            advance(k)

    def mark():
        for k in MARKS[state["mark"]]:
            if k in live:
                advance(k)
        state["mark"] += 1

    def feed_start(l, middle):
        f = norm(middle, p(l, 2), p(l, 3))
        f_v[...] = f.astype(BF16)
        ft_v[...] = f.T.astype(BF16)
        dacc[...] = jnp.zeros_like(dacc)

    def feed_both(l, total, between):
        we, wr = we_v.at[l], wr_v.at[l]

        def step(j, carry):
            at = pl.multiple_of(j * CH, CH)
            part, to = lax.div(j, PART // CH), pl.multiple_of(lax.rem(j, PART // CH) * CH, CH)
            dy = cot_v[...]
            hidden, slope = gelu_both(expand_step(j, f_v, we, p_v.at[l]))
            hidden = hidden.astype(BF16)
            if total is not None:
                total[...] += dot(hidden, wr[pl.ds(at, CH), :])
            gff[l, part, pl.ds(pl.multiple_of(PART + to, CH), CH), :] = dot_tn(hidden, dy).astype(BF16)
            dpre = (dot_nt(dy, wr[pl.ds(at, CH), :]) * slope).astype(BF16)
            deb[l, pl.ds(j, 1), :] = jnp.sum(dpre.astype(F32), axis=0, keepdims=True)
            gff[l, part, pl.ds(to, CH), :] = dot(ft_v[...], dpre).astype(BF16)
            dacc[...] += dot_nt(dpre, we[:, pl.ds(at, CH)])
            for k, work in between.items():
                pl.when(j == k)(work)
            return carry

        lax.fori_loop(0, FF // CH, step, 0)

    def feed_end(l, middle):
        dend = cot_v[...].astype(F32)
        dmid, dgain, dbias = norm_back(dacc[...], middle, p(l, 2))
        return dmid + dend, [dgain, dbias, jnp.sum(dend, axis=0, keepdims=True)]

    swapped("p", "sm", "we", "wr")
    acc[...] = mid_v[2] + p(1, 4)
    feed_start(1, mid_v[2])
    feed_both(1, acc, {1: lambda: begin(0)})
    begin(1)
    out_v[...] = acc[...].astype(BF16)
    acc[...], feed_small = feed_end(1, mid_v[2])
    mark()
    own_rows = act_out.at[pl.ds(own_at, T)]
    out_near = pltpu.make_async_copy(out_v, own_rows, out_sem.at[2])
    out_away = remote(out_v, own_rows, out_send.at[0], out_recv.at[0])
    pl.when(sec == 1)(out_near.start)
    pl.when(sec == 0)(out_away.start)

    def narrow_tail(l, rows):
        at = 2 * D + l * NARROW + NARROW - 16
        gd_v[at : at + 16, :] = small_rows(rows).astype(BF16)

    dc, dmem = mixture_bwd(
        acc[...].astype(BF16), low_v[1], mem_v[...], experts_of(xp_v, 2), xw, same_of(s_ends, t_ends), kept[1],
        gx_v, 0, gd_v, 2 * D + 2 * NARROW, mark,
    )
    cot_v[...] = dmem.astype(BF16)
    dbefore, dgain, dbias = norm_back(dc, mid_v[1], xp_v[0:1, :])
    narrow_tail(2, [dgain, dbias])
    mid_v[2] = acc[...] + dbefore
    begin(2)
    mark()

    def self_fwd(l, with_out):
        x = x_v[l].astype(F32)
        a = norm(x, p(l, 0), p(l, 1)).astype(BF16)
        low_v[0] = a
        at = 9 + 2 * sec
        experts = [laid_out(p_v[l, pl.ds(at + r, 1), :]) for r in range(2)]
        ends = t_ends if l else s_ends
        allowed = same_of(ends, ends)
        allowed = allowed & earlier() if l else allowed
        out = mixture_fwd(a, a, experts, weights(l, sm_v.at[l]), allowed, kept[0], with_out)
        return x + out if with_out else None

    def self_back(l, grad, wide, feed_small):
        at = 9 + 2 * sec
        experts = [laid_out(p_v[l, pl.ds(at + r, 1), :]) for r in range(2)]
        ends = t_ends if l else s_ends
        allowed = same_of(ends, ends)
        allowed = allowed & earlier() if l else allowed
        da, ds = mixture_bwd(
            grad[...].astype(BF16), low_v[0], low_v[0], experts, weights(l, sm_v.at[l]), allowed, kept[0],
            wide, 0, gd_v, 2 * D + l * NARROW, mark,
        )
        dx, dgain, dbias = norm_back(da + ds, x_v[l].astype(F32), p(l, 0))
        mid_v[l] = grad[...] + dx
        narrow_tail(l, [dgain, dbias] + feed_small + [deb[l, i : i + 1, :] for i in range(FF // D)])

    swapped("wq", "wo", "x")
    lay_small(1 - sec, sm_v.at[1 - sec])
    mid_v[0] = self_fwd(0, True)
    mark()
    feed_start(0, mid_v[0])
    feed_both(0, None, {1: lambda: begin(3)})
    begin(4)
    acc[...], own_small = feed_end(0, mid_v[0])
    mark()
    self_back(0, acc, ge_v, own_small)
    begin(5)
    mark()

    self_fwd(1, False)
    mark()
    self_back(1, mid_v.at[2], gd_v, feed_small)
    at = 2 * D + 3 * NARROW
    gd_v[at:, :] = jnp.zeros((2 * halves[6] - at, D), BF16)
    begin(6)
    gin_rows = gin_out.at[pl.ds(own_at, T)]
    gin_near = pltpu.make_async_copy(mid_v.at[sec], gin_rows, out_sem.at[13])
    gin_away = remote(mid_v.at[1 - sec], gin_rows, out_send.at[1], out_recv.at[1])
    gin_near.start()
    gin_away.start()
    mark()
    mark()
    while live:
        for k in list(live):
            advance(k)
    for wait in finals:
        wait()
    gin_near.wait()
    gin_away.wait()

    @pl.when(sec == 0)
    def _():
        out_away.wait_send()
        for copy in memory_out:
            copy.wait()

    @pl.when(sec == 1)
    def _():
        out_away.wait_recv()
        out_near.wait()


def widen(act, gin, gff, gat, gx, *refs):
    outs, (act_v, gin_v, gff_v, gat_v, gx_v, ex_v, re_v, mats, in_sem, out_sem) = refs[:-10], refs[-10:]
    act_out, gin_out, expand, reduce, q, o, xq, xo = outs[:8]
    smalls = outs[8:]
    loads, at = [], 0
    for ref, dst in ((gff, gff_v), (gat, gat_v), (gx, gx_v)):
        for first in range(0, ref.shape[0], D):
            rows = pl.ds(first, min(D, ref.shape[0] - first))
            loads.append(pltpu.make_async_copy(ref.at[rows], dst.at[rows], in_sem.at[at]))
            loads[-1].start()
            at += 1
    passing = [
        pltpu.make_async_copy(a, b, in_sem.at[at + i]) for i, (a, b) in enumerate(((act, act_v), (gin, gin_v)))
    ]
    for copy in passing:
        copy.start()
    stores = []

    def store(src, dst):
        stores.append(pltpu.make_async_copy(src, dst, out_sem.at[len(stores)]))
        stores[-1].start()

    blocks = PART // D
    for i in range(2 * FF // D):
        loads[i].wait()
        part, kind, block = i // (2 * blocks), (i // blocks) % 2, i % blocks
        col = part * PART + block * D
        value = gff_v[i * D : (i + 1) * D, :].astype(F32)
        if kind == 0:
            ex_v[:, col : col + D] = value
            store(ex_v.at[:, pl.ds(col, D)], expand.at[:, pl.ds(col, D)])
        else:
            re_v[col : col + D, :] = value
            store(re_v.at[pl.ds(col, D)], reduce.at[pl.ds(col, D)])
    i = 2 * FF // D
    for m, (src, row, dst) in enumerate(((gat_v, 0, q), (gat_v, D, o), (gx_v, 0, xq), (gx_v, D, xo))):
        loads[i + m + m // 2].wait()
        mats[m] = src[row : row + D, :].astype(F32)
        store(mats.at[m], dst)
    for k, load in enumerate((loads[i + 2], loads[i + 5])):
        load.wait()
        src = (gat_v, gx_v)[k]
        ks, vs, rs = smalls[:3] if k == 0 else smalls[9:12]
        at = 2 * D
        ks[...] = src[at : at + 64, :].astype(F32)
        vs[...] = src[at + 64 : at + PAIR, :].astype(F32)
        rs[...] = src[at + PAIR : at + PAIR + 16, :].astype(F32)[0:8]
        tail = src[at + PAIR + 16 : at + NARROW, :].astype(F32)
        if k == 0:
            for j in range(5):
                smalls[3 + j][...] = tail[j : j + 1]
            for j in range(FF // D):
                smalls[8][:, j * D : (j + 1) * D] = tail[5 + j : 6 + j]
        else:
            for j in range(2):
                smalls[12 + j][...] = tail[j : j + 1]
    for copy, src, dst in zip(passing, (act_v, gin_v), (act_out, gin_out)):
        copy.wait()
        store(src, dst)
    for copy in stores:
        copy.wait()


def body(n, *arrays):
    (
        embeddings, cotangent, source_lengths, target_lengths, self_routes, cross_routes,
        attend_gain, attend_bias, self_router, query_weight, key_weight, value_weight, output_weight,
        feed_gain, feed_bias, expand_weight, expand_bias, reduce_weight, reduce_bias,
        cross_gain, cross_bias, cross_router, cross_query, cross_key, cross_value, cross_output,
    ) = arrays
    row_count = embeddings.shape[1]
    sents = source_lengths.shape[1]
    part = up(PART, n)
    halves = (part, part, up(D, n), part, part, up(D, n), up((2 * D + 3 * NARROW + 1) // 2, n))
    cut = [stream for i, half in enumerate(halves) for stream in streams_of(i, half, n)]
    streams, lands = len(cut), sum(stream[2] for stream in cut)
    steps = n.bit_length() - 1 + scattered(n) + 2
    S, V, DMA = jax.ShapeDtypeStruct, pltpu.VMEM, pltpu.SemaphoreType.DMA
    hbm, smem = pl.BlockSpec(memory_space=pl.ANY), pl.BlockSpec(memory_space=pltpu.SMEM)
    vmem = pl.BlockSpec(memory_space=pltpu.VMEM)
    rows = 2 * D + NARROW
    act, gin, gff, gat, gx = pl.pallas_call(
        functools.partial(fused, n, halves, sents),
        in_specs=[smem] * 2 + [vmem] * 16 + [hbm] * 8,
        out_specs=[hbm] * 5,
        out_shape=[
            S((row_count, D), BF16), S((row_count, D), F32),
            S((2 * FF, D), BF16), S((rows, D), BF16), S((rows, D), BF16),
        ],
        scratch_shapes=[
            V((3, T, D), BF16), V((2, 16, D), F32), V((16, D), F32), V((2, NARROW, D), BF16), V((NARROW, D), BF16),
            V((2, D, D), BF16), V((2, D, D), BF16), V((2, D, FF), BF16), V((2, FF, D), BF16),
            V((T, D), BF16), V((D, D), BF16), V((D, D), BF16),
            V((3, 3, PAIR, D), BF16), [[V(s, t) for _, s, t in KEPT] for _ in range(2)],
            V((2, T, D), BF16), V((3, T, D), F32), V((T, D), BF16), V((T, D), BF16), V((T, D), BF16), V((D, T), BF16),
            V((2, T, D), F32), V((2, 8, D), F32), V((T, D), BF16),
            V((2, PARTS, 2 * part, D), BF16), *(V((2 * halves[i], D), BF16) for i in (2, 5, 6)),
            V((2, max(halves), D), BF16), V((lands, D), BF16), DMA((streams,)), DMA((streams, steps)),
            pltpu.SemaphoreType.REGULAR((streams, 1 + scattered(n))),
            DMA((9,)), DMA((9,)), DMA((9,)), DMA((14,)), DMA((2,)), DMA((2,)),
        ],
        compiler_params=pltpu.CompilerParams(
            collective_id=0, has_side_effects=True, vmem_limit_bytes=(63 << 20) + (900 << 10)
        ),
    )(
        source_lengths, target_lengths, self_routes[0].T, cross_routes.T,
        attend_gain, attend_bias, feed_gain, feed_bias, reduce_bias, expand_bias,
        key_weight[0].T, value_weight[0].T, self_router[0].T,
        cross_gain[None], cross_bias[None], cross_key.T, cross_value.T, cross_router.T,
        embeddings[0], cotangent, query_weight[0], output_weight[0], expand_weight[0], reduce_weight[0],
        cross_query, cross_output,
    )
    wide = [(row_count, D), (row_count, D), (D, FF), (FF, D)] + [(D, D)] * 4
    narrow = [(64, D), (64, D), (8, D)] + [(1, D)] * 5 + [(1, FF)] + [(64, D), (64, D), (8, D)] + [(1, D)] * 2
    out = pl.pallas_call(
        widen,
        in_specs=[hbm] * 5,
        out_specs=[hbm] * len(wide) + [vmem] * len(narrow),
        out_shape=[S(s, BF16 if i == 0 else F32) for i, s in enumerate(wide + narrow)],
        scratch_shapes=[
            V((row_count, D), BF16), V((row_count, D), F32), V((2 * FF, D), BF16), V((rows, D), BF16), V((rows, D), BF16),
            V((D, FF), F32), V((FF, D), F32), V((4, D, D), F32), DMA((2 * FF // D + 8,)), DMA((2 * FF // D + 6,)),
        ],
        compiler_params=pltpu.CompilerParams(vmem_limit_bytes=(63 << 20) + (900 << 10)),
    )(act, gin, gff, gat, gx)
    act, gin, expand, reduce, q, o, xq, xo = out[:8]
    k, v, r, gains, biases, fgain, fbias, rbias, ebias, xk, xv, xr, xgain, xbias = out[8:]
    return (
        act[None], gin[None], gains, biases, r.T[None], q[None], k.T[None], v.T[None], o[None],
        fgain, fbias, expand[None], ebias, reduce[None], rbias,
        xgain[0], xbias[0], xr.T, xq, xk.T, xv.T, xo,
    )


def solution(mesh):
    n = mesh.shape["dp"]
    stacked, rows = P("section", None), P("dp", None)
    matrix, both = P("section", None, None), P("section", "dp", None)
    params = (
        stacked, stacked, matrix, matrix, matrix, matrix, matrix, stacked, stacked, matrix, stacked, matrix, stacked,
    ) + (P(),) * 7
    return jax.shard_map(
        functools.partial(body, n),
        mesh=mesh,
        in_specs=(both, rows, rows, rows, both, rows) + params,
        out_specs=(both, both) + params,
        check_vma=False,
    )
```

profile of v0, /device:TPU:1, one launch (start us, length us, event | category | flops | bytes accessed | tf_op | source)
XLA Modules:
  0.0 151.6 jit_solution(3327788126658254367)
XLA Ops:
  0.7 140.3 %shard_map.417 = (bf16[1024,512]{1,0:T(8,128)(2,1)}, f32[1024,512]{1,0:T(8,128)}, bf16[4096,512]{1,0:T(8,128)(2,1)}, bf16[1184,512]{1,0:T(8,128)(2,1)}, bf16[1184,512]{1,0:T(8,128)(2,1)}) custom-call(s32[2,8]{1,0:T(2,128)} %refs_0_.1, s32[2,8]{1,0:T(2,128)} %refs_1_.1, s32[2,1024]{1,0:T(2,128)} %bitcast.52, s32[2,1024]{1,0:T(2,128)} %bitcast.53, ...), custom_call_target="tpu_custom_call" | custom-call | tf_op jit(solution)/shard_map/pallas_call | solution.py:847
  140.9 10.5 %shard_map.418 = (bf16[1024,512]{1,0:T(8,128)(2,1)}, f32[1024,512]{1,0:T(8,128)}, f32[512,2048]{1,0:T(8,128)}, f32[2048,512]{1,0:T(8,128)}, f32[512,512]{1,0:T(8...) custom-call(bf16[1024,512]{1,0:T(8,128)(2,1)} %get-tuple-element.49., ...), custom_call_target="tpu_custom_call" | custom-call | tf_op jit(solution)/shard_map/pallas_call | solution.py:880
where the time goes:
time: 152 us
  Pallas kernels  151 us (99%)
    pallas_call x1, Pallas kernels, body(): pl.pallas_call(functools.partial(fused, n, halves, sents), in_specs=[smem...  140 us
    pallas_call x1, Pallas kernels, body(): pl.pallas_call(widen, in_specs=[hbm] * 5, out_specs=[hbm] * len(wide) + [...  10.5 us

commit v1 on v0

--- a/solution.py
+++ b/solution.py
@@ -209,12 +209,11 @@
     return dot(f[...], we[:, pl.ds(at, CH)]) + p[pl.ds(5 + j, 1), :]
 
 
-def feed_fwd(pairs, we, p, wr):
+def feed_fwd(f, acc, we, p, wr, ready):
     def step(j, carry):
-        at = pl.multiple_of(j * CH, CH)
-        for f, acc in pairs:
-            hidden = gelu(expand_step(j, f, we, p)).astype(BF16)
-            acc[...] += dot(hidden, wr[pl.ds(at, CH), :])
+        ready(j)
+        hidden = gelu(expand_step(j, f, we, p)).astype(BF16)
+        acc[...] += dot(hidden, wr[pl.ds(pl.multiple_of(j * CH, CH), CH), :])
         return carry
 
     lax.fori_loop(0, FF // CH, step, 0)
@@ -266,35 +265,35 @@
 
 
 PLAN = (
-    ((1, (1, 0, 2, 3)), (2, (2, 0, 1, 3)), (1, (0, 3, 1, 2))),
-    ((1, (0, 1, 2, 3)), (2, (0, 1, 2, 3)), (1, (1, 3, 2, 0))),
-    ((1, (1, 0, 2, 3)), (1, (3, 0, 1, 2))),
-    ((2, (0, 1, 2, 3)), (1, (1, 3, 0, 2)), (1, (0, 1, 2, 3))),
-    ((1, (1, 0, 2, 3)), (2, (2, 0, 1, 3)), (1, (0, 1, 2, 3))),
-    ((1, (1, 0, 2, 3)), (1, (2, 1, 0, 3))),
-    ((1, (1, 0, 3, 2)), (1, (0, 1, 2, 3)), (1, (0, 1, 2, 3))),
+    ((1, (1, 0, 2, 3)), (2, (1, 0, 2, 3)), (1, (0, 1, 2, 3))),
+    ((1, (2, 0, 1, 3)), (1, (0, 1, 2, 3)), (2, (0, 1, 2, 3))),
+    ((1, (2, 1, 0, 3)), (1, (1, 2, 0, 3))),
+    ((2, (2, 0, 1, 3)), (1, (1, 0, 2, 3)), (1, (1, 0, 2, 3))),
+    ((1, (2, 0, 1, 3)), (1, (0, 1, 2, 3)), (2, (0, 1, 2, 3))),
+    ((1, (1, 0, 2, 3)), (1, (2, 0, 1, 3))),
+    ((1, (1, 0, 2, 3)), (1, (1, 0, 2, 3)), (1, (0, 1, 2, 3))),
 )
 MARKS = (
     (),
     (),
     (),
-    (0,),
-    (2,),
-    (1, 3, 5, 2, 4, 0, 6),
-    (7, 11, 12, 13),
+    (0, 2),
+    (1, 3, 2, 4, 5, 6, 0, 7),
+    (11, 12, 13),
     (9,),
-    (3, 0, 2, 8, 5),
-    (4, 10),
-    (14, 15, 11, 1),
-    (12, 6, 3),
-    (7, 8, 2, 9, 10, 0, 5, 13, 4, 11, 14),
+    (1, 8, 10, 2, 3, 0, 4),
+    (7, 12, 5),
+    (11, 6, 3, 1, 2),
+    (0, 4, 14, 15, 13, 12, 5, 9),
+    (3,),
+    (8, 1, 2, 10, 0, 7, 4, 11),
     (
-        15, 1, 6, 16, 12, 17, 3, 18, 7, 9, 8, 5, 2, 10, 13, 0, 14, 11, 15, 4, 7, 1, 9, 6,
-        17, 16, 3, 13, 12, 8, 2, 0, 10, 18, 14, 5, 17, 7, 11, 15, 9, 4, 16, 3, 18, 1, 0, 7,
-        5, 6, 9, 13, 17, 3, 12, 1, 8, 7, 4, 18, 0, 2, 6, 10, 3, 14, 11, 0, 4, 15, 8, 1,
-        3, 16, 10, 11, 2, 5, 6, 8, 2, 9, 10, 13, 17, 12, 5, 4, 11, 5, 6, 4, 1, 6, 7, 16,
-        9, 18, 13, 14, 12, 1, 15, 8, 7, 17, 9, 16, 18, 11, 14, 10, 8, 13, 17, 11, 16, 18, 10, 12,
-        15, 17, 14, 18, 15, 13, 16, 13, 14, 12, 17, 14, 12, 15, 16, 17, 18, 15, 16, 18,
+        14, 6, 15, 12, 16, 17, 18, 13, 5, 9, 3, 8, 2, 11, 1, 10, 14, 0, 7, 15, 4, 6, 16, 12,
+        13, 18, 5, 9, 17, 0, 1, 3, 8, 16, 11, 14, 2, 10, 15, 4, 7, 17, 6, 18, 12, 5, 13, 1,
+        9, 0, 16, 3, 8, 4, 11, 17, 0, 14, 10, 18, 2, 15, 5, 12, 7, 6, 9, 13, 2, 16, 4, 3,
+        17, 1, 4, 10, 14, 18, 8, 3, 15, 11, 7, 1, 12, 5, 13, 16, 6, 9, 14, 17, 15, 18, 5, 10,
+        16, 7, 8, 6, 7, 11, 17, 13, 18, 6, 12, 9, 14, 12, 9, 15, 10, 8, 16, 18, 10, 17, 8, 11,
+        14, 11, 15, 14, 16, 13, 15, 16, 17, 13, 18, 17, 18,
     ),
 )
 
@@ -413,7 +412,7 @@
         emb, cot, wq, wo, we, wr, xwq, xwo,
         act_out, gin_out, gff_out, gat_out, gx_out,
         x_v, p_v, xp_v, sm_v, xsm_v, wq_v, wo_v, we_v, wr_v, cot_v, xwq_v, xwo_v,
-        wsm, kept_refs, low_v, mid_v, mem_v, stage_v, f_v, ft_v, totals, deb, out_v,
+        wsm, kept_refs, low_v, mid_v, mem_v, f_v, ft_v, totals, deb, out_v,
         gff, gx_v, ge_v, gd_v, twin_in, ring_in, sum_send, sum_recv, sum_free,
         own_sem, in_send, in_recv, out_sem, out_send, out_recv,
     ) = refs
@@ -498,17 +497,30 @@
         @pl.when(i == 0)
         def _():
             pl.semaphore_wait(barrier, here.bits + 1)
-            for name in ("p", "sm", "we", "wr", "wq", "wo", "x"):
+            for name in ("middle", "p", "sm"):
+                swaps[name].start()
+            for j in range(FF // CH):
+                for copy in feed_swaps(j):
+                    copy.start()
+            for name in ("wq", "wo", "x"):
                 swaps[name].start()
 
         return carry
 
     swaps = {}
     for i, (name, src, dst) in enumerate((
-        ("p", p_v.at[sec], p_v), ("sm", sm_v.at[sec], sm_v), ("we", we, we_v), ("wr", wr, wr_v), ("wq", wq, wq_v),
-        ("wo", wo, wo_v), ("x", slot(emb, 1 - sec), x_v),
+        ("p", p_v.at[sec], p_v), ("sm", sm_v.at[sec], sm_v), ("wq", wq, wq_v), ("wo", wo, wo_v),
+        ("x", slot(emb, 1 - sec), x_v), ("middle", dacc, mid_v),
     )):
         swaps[name] = remote(src, dst.at[sec], in_send.at[i], in_recv.at[i])
+
+    def feed_swaps(j):
+        rows = pl.ds(pl.multiple_of(j * CH, CH), CH)
+        first = len(swaps) + 2 * j
+        return (
+            remote(we.at[:, rows], we_v.at[sec, :, rows], in_send.at[first], in_recv.at[first]),
+            remote(wr.at[rows], wr_v.at[sec, rows], in_send.at[first + 1], in_recv.at[first + 1]),
+        )
 
     def swapped(*names):
         for name in names:
@@ -517,52 +529,46 @@
     need("x_oth", "x", "wq", "wo")
     lax.fori_loop(0, 2, own_middle, 0)
     need("we", "wr")
-    middle_away = remote(dacc, mid_v.at[1], in_send.at[7], in_recv.at[7])
-    memory_away = remote(stage_v, mem_v, in_send.at[8], in_recv.at[8])
-
-    @pl.when(sec == 0)
-    def _():
-        for f, total in ((f_v, acc), (stage_v, dacc)):
-            middle = total[...]
-            f[...] = norm(middle, p(0, 2), p(0, 3)).astype(BF16)
-            total[...] = middle + p(0, 4)
-        feed_fwd(((f_v, acc), (stage_v, dacc)), we_v.at[0], p_v.at[0], wr_v.at[0])
-        stage_v[...] = dacc[...].astype(BF16)
-        memory_away.start()
-        mem_v[...] = acc[...].astype(BF16)
-
-    @pl.when(sec == 1)
-    def _():
-        middle_away.start()
-        mid_v[1] = acc[...]
-
+    mid_v[sec] = acc[...]
+    swapped("middle", "p", "sm")
+    f_v[...] = norm(mid_v[0], p(0, 2), p(0, 3)).astype(BF16)
+    acc[...] = mid_v[0] + p(0, 4)
+
+    def feed_ready(j):
+        for copy in feed_swaps(j):
+            copy.wait()
+
+    feed_fwd(f_v, acc, we_v.at[0], p_v.at[0], wr_v.at[0], feed_ready)
+    mem_v[...] = acc[...].astype(BF16)
+    lay_small(1 - sec, sm_v.at[1 - sec])
     need("xwq", "xwo", "cot")
     lay_small(2, xsm_v)
-
-    @pl.when(sec == 0)
-    def _():
-        middle_away.wait_recv()
-        memory_away.wait_send()
-
-    @pl.when(sec == 1)
-    def _():
-        memory_away.wait_recv()
-        middle_away.wait_send()
-
     finals = []
 
     def hand_out(start, end):
         start()
         finals.append(end)
 
-    memory_out = [
-        pltpu.make_async_copy(ref, act_out.at[pl.ds(m * T, T)], out_sem.at[m]) for m, ref in enumerate((mem_v, stage_v))
-    ]
-
-    @pl.when(sec == 0)
-    def _():
-        for copy in memory_out:
-            copy.start()
+    own_rows = act_out.at[pl.ds(own_at, T)]
+    rows_out = []
+    for i, ref in enumerate((mem_v, out_v)):
+        near = pltpu.make_async_copy(ref, own_rows, out_sem.at[i])
+        away = remote(ref, own_rows, out_send.at[i], out_recv.at[i])
+        rows_out.append((near, away))
+
+    def rows_start(i):
+        pl.when(sec == i)(rows_out[i][0].start)
+        pl.when(sec != i)(rows_out[i][1].start)
+
+    def rows_end(i):
+        pl.when(sec != i)(rows_out[i][1].wait_send)
+
+        @pl.when(sec == i)
+        def _():
+            rows_out[i][0].wait()
+            rows_out[i][1].wait_recv()
+
+    rows_start(0)
 
     s_ends, t_ends = (ends_of([ref[sec, i] for i in range(sents)]) for ref in (sl, tl))
     xw = (xwq_v, wsm.at[2, 0], wsm.at[2, 1], xsm_v.at[pl.ds(0, PAIR)], wsm.at[2, 2], xwo_v)
@@ -662,7 +668,6 @@
         dmid, dgain, dbias = norm_back(dacc[...], middle, p(l, 2))
         return dmid + dend, [dgain, dbias, jnp.sum(dend, axis=0, keepdims=True)]
 
-    swapped("p", "sm", "we", "wr")
     acc[...] = mid_v[2] + p(1, 4)
     feed_start(1, mid_v[2])
     feed_both(1, acc, {1: lambda: begin(0)})
@@ -670,11 +675,7 @@
     out_v[...] = acc[...].astype(BF16)
     acc[...], feed_small = feed_end(1, mid_v[2])
     mark()
-    own_rows = act_out.at[pl.ds(own_at, T)]
-    out_near = pltpu.make_async_copy(out_v, own_rows, out_sem.at[2])
-    out_away = remote(out_v, own_rows, out_send.at[0], out_recv.at[0])
-    pl.when(sec == 1)(out_near.start)
-    pl.when(sec == 0)(out_away.start)
+    rows_start(1)
 
     def narrow_tail(l, rows):
         at = 2 * D + l * NARROW + NARROW - 16
@@ -691,7 +692,7 @@
     begin(2)
     mark()
 
-    def self_fwd(l, with_out):
+    def self_fwd(l):
         x = x_v[l].astype(F32)
         a = norm(x, p(l, 0), p(l, 1)).astype(BF16)
         low_v[0] = a
@@ -700,8 +701,7 @@
         ends = t_ends if l else s_ends
         allowed = same_of(ends, ends)
         allowed = allowed & earlier() if l else allowed
-        out = mixture_fwd(a, a, experts, weights(l, sm_v.at[l]), allowed, kept[0], with_out)
-        return x + out if with_out else None
+        mixture_fwd(a, a, experts, weights(l, sm_v.at[l]), allowed, kept[0], False)
 
     def self_back(l, grad, wide, feed_small):
         at = 9 + 2 * sec
@@ -717,20 +717,19 @@
         mid_v[l] = grad[...] + dx
         narrow_tail(l, [dgain, dbias] + feed_small + [deb[l, i : i + 1, :] for i in range(FF // D)])
 
-    swapped("wq", "wo", "x")
-    lay_small(1 - sec, sm_v.at[1 - sec])
-    mid_v[0] = self_fwd(0, True)
-    mark()
     feed_start(0, mid_v[0])
     feed_both(0, None, {1: lambda: begin(3)})
     begin(4)
     acc[...], own_small = feed_end(0, mid_v[0])
     mark()
+    swapped("wq", "wo", "x")
+    self_fwd(0)
+    mark()
     self_back(0, acc, ge_v, own_small)
     begin(5)
     mark()
 
-    self_fwd(1, False)
+    self_fwd(1)
     mark()
     self_back(1, mid_v.at[2], gd_v, feed_small)
     at = 2 * D + 3 * NARROW
@@ -738,7 +737,7 @@
     begin(6)
     gin_rows = gin_out.at[pl.ds(own_at, T)]
     gin_near = pltpu.make_async_copy(mid_v.at[sec], gin_rows, out_sem.at[13])
-    gin_away = remote(mid_v.at[1 - sec], gin_rows, out_send.at[1], out_recv.at[1])
+    gin_away = remote(mid_v.at[1 - sec], gin_rows, out_send.at[2], out_recv.at[2])
     gin_near.start()
     gin_away.start()
     mark()
@@ -751,16 +750,8 @@
     gin_near.wait()
     gin_away.wait()
 
-    @pl.when(sec == 0)
-    def _():
-        out_away.wait_send()
-        for copy in memory_out:
-            copy.wait()
-
-    @pl.when(sec == 1)
-    def _():
-        out_away.wait_recv()
-        out_near.wait()
+    rows_end(0)
+    rows_end(1)
 
 
 def widen(act, gin, gff, gat, gx, *refs):
@@ -857,12 +848,12 @@
             V((2, D, D), BF16), V((2, D, D), BF16), V((2, D, FF), BF16), V((2, FF, D), BF16),
             V((T, D), BF16), V((D, D), BF16), V((D, D), BF16),
             V((3, 3, PAIR, D), BF16), [[V(s, t) for _, s, t in KEPT] for _ in range(2)],
-            V((2, T, D), BF16), V((3, T, D), F32), V((T, D), BF16), V((T, D), BF16), V((T, D), BF16), V((D, T), BF16),
+            V((2, T, D), BF16), V((3, T, D), F32), V((T, D), BF16), V((T, D), BF16), V((D, T), BF16),
             V((2, T, D), F32), V((2, 8, D), F32), V((T, D), BF16),
             V((2, PARTS, 2 * part, D), BF16), *(V((2 * halves[i], D), BF16) for i in (2, 5, 6)),
             V((2, max(halves), D), BF16), V((lands, D), BF16), DMA((streams,)), DMA((streams, steps)),
             pltpu.SemaphoreType.REGULAR((streams, 1 + scattered(n))),
-            DMA((9,)), DMA((9,)), DMA((9,)), DMA((14,)), DMA((2,)), DMA((2,)),
+            DMA((9,)), DMA((6 + 2 * FF // CH,)), DMA((6 + 2 * FF // CH,)), DMA((14,)), DMA((3,)), DMA((3,)),
         ],
         compiler_params=pltpu.CompilerParams(
             collective_id=0, has_side_effects=True, vmem_limit_bytes=(63 << 20) + (900 << 10)

time: 152 us -> 142 us (0.934)
  Pallas kernels: 151 us -> 141 us
    pallas_call x1, Pallas kernels: 140 us -> 130 us  [body(): pl.pallas_call(functools.partial(fused, n, halves, sents), in_specs=[smem...]
where the time goes in v1:
time: 142 us
  Pallas kernels  141 us (99%)
    pallas_call x1, Pallas kernels, body(): pl.pallas_call(functools.partial(fused, n, halves, sents), in_specs=[smem...  130 us
    pallas_call x1, Pallas kernels, body(): pl.pallas_call(widen, in_specs=[hbm] * 5, out_specs=[hbm] * len(wide) + [...  10.5 us

profile of v1, /device:TPU:1, one launch (start us, length us, event | category | flops | bytes accessed | tf_op | source)
XLA Modules:
  0.0 141.8 jit_solution(2502481578699958070)
XLA Ops:
  0.7 130.4 %shard_map.417 = (bf16[1024,512]{1,0:T(8,128)(2,1)}, f32[1024,512]{1,0:T(8,128)}, bf16[4096,512]{1,0:T(8,128)(2,1)}, bf16[1184,512]{1,0:T(8,128)(2,1)}, bf16[1184,512]{1,0:T(8,128)(2,1)}) custom-call(s32[2,8]{1,0:T(2,128)} %refs_0_.1, s32[2,8]{1,0:T(2,128)} %refs_1_.1, s32[2,1024]{1,0:T(2,128)} %bitcast.52, s32[2,1024]{1,0:T(2,128)} %bitcast.53, ...), custom_call_target="tpu_custom_call" | custom-call | tf_op jit(solution)/shard_map/pallas_call | solution.py:838
  131.1 10.5 %shard_map.418 = (bf16[1024,512]{1,0:T(8,128)(2,1)}, f32[1024,512]{1,0:T(8,128)}, f32[512,2048]{1,0:T(8,128)}, f32[2048,512]{1,0:T(8,128)}, f32[512,512]{1,0:T(8...) custom-call(bf16[1024,512]{1,0:T(8,128)(2,1)} %get-tuple-element.49., ...), custom_call_target="tpu_custom_call" | custom-call | tf_op jit(solution)/shard_map/pallas_call | solution.py:871

commit v2 on v1

--- a/solution.py
+++ b/solution.py
@@ -758,24 +758,27 @@
     outs, (act_v, gin_v, gff_v, gat_v, gx_v, ex_v, re_v, mats, in_sem, out_sem) = refs[:-10], refs[-10:]
     act_out, gin_out, expand, reduce, q, o, xq, xo = outs[:8]
     smalls = outs[8:]
-    loads, at = [], 0
+    passing = [
+        pltpu.make_async_copy(a, b, in_sem.at[i]) for i, (a, b) in enumerate(((act, act_v), (gin, gin_v)))
+    ]
+    for copy in passing:
+        copy.start()
+    loads, at = [], len(passing)
     for ref, dst in ((gff, gff_v), (gat, gat_v), (gx, gx_v)):
         for first in range(0, ref.shape[0], D):
             rows = pl.ds(first, min(D, ref.shape[0] - first))
             loads.append(pltpu.make_async_copy(ref.at[rows], dst.at[rows], in_sem.at[at]))
             loads[-1].start()
             at += 1
-    passing = [
-        pltpu.make_async_copy(a, b, in_sem.at[at + i]) for i, (a, b) in enumerate(((act, act_v), (gin, gin_v)))
-    ]
-    for copy in passing:
-        copy.start()
     stores = []
 
     def store(src, dst):
         stores.append(pltpu.make_async_copy(src, dst, out_sem.at[len(stores)]))
         stores[-1].start()
 
+    for copy, src, dst in zip(passing, (act_v, gin_v), (act_out, gin_out)):
+        copy.wait()
+        store(src, dst)
     blocks = PART // D
     for i in range(2 * FF // D):
         loads[i].wait()
@@ -810,9 +813,6 @@
         else:
             for j in range(2):
                 smalls[12 + j][...] = tail[j : j + 1]
-    for copy, src, dst in zip(passing, (act_v, gin_v), (act_out, gin_out)):
-        copy.wait()
-        store(src, dst)
     for copy in stores:
         copy.wait()
 

time: 142 us -> 141 us (level)
  no operation moved by 1% of the time
where the time goes in v2:
time: 141 us
  Pallas kernels  140 us (99%)
    pallas_call x1, Pallas kernels, body(): pl.pallas_call(functools.partial(fused, n, halves, sents), in_specs=[smem...  130 us
    pallas_call x1, Pallas kernels, body(): pl.pallas_call(widen, in_specs=[hbm] * 5, out_specs=[hbm] * len(wide) + [...  9.25 us

profile of v2, /device:TPU:1, one launch (start us, length us, event | category | flops | bytes accessed | tf_op | source)
XLA Modules:
  0.0 140.5 jit_solution(16123504560608101122)
XLA Ops:
  0.7 130.4 %shard_map.417 = (bf16[1024,512]{1,0:T(8,128)(2,1)}, f32[1024,512]{1,0:T(8,128)}, bf16[4096,512]{1,0:T(8,128)(2,1)}, bf16[1184,512]{1,0:T(8,128)(2,1)}, bf16[1184,512]{1,0:T(8,128)(2,1)}) custom-call(s32[2,8]{1,0:T(2,128)} %refs_0_.1, s32[2,8]{1,0:T(2,128)} %refs_1_.1, s32[2,1024]{1,0:T(2,128)} %bitcast.52, s32[2,1024]{1,0:T(2,128)} %bitcast.53, ...), custom_call_target="tpu_custom_call" | custom-call | tf_op jit(solution)/shard_map/pallas_call | solution.py:838
  131.1 9.3 %shard_map.418 = (bf16[1024,512]{1,0:T(8,128)(2,1)}, f32[1024,512]{1,0:T(8,128)}, f32[512,2048]{1,0:T(8,128)}, f32[2048,512]{1,0:T(8,128)}, f32[512,512]{1,0:T(8...) custom-call(bf16[1024,512]{1,0:T(8,128)(2,1)} %get-tuple-element.49., ...), custom_call_target="tpu_custom_call" | custom-call | tf_op jit(solution)/shard_map/pallas_call | solution.py:871
